TPU v7x, 32 devices: a whole 2x2x4 slice. The times are simulated.
32 devices in a mesh: ty: 4 (over x, core), tx: 4 (over z), mode: 2 (over y).
Axes of the slice: x: 2, y: 2, z: 4, core: 2. Of those that a mesh axis runs over, the one named last changes fastest.
Arguments:
- object_field: float32 [2, 2, 1024, 1024], P(None, None, 'ty', 'tx'), may hold values from -2.4 to 2.4
- probe: float32 [4, 256, 512], P('mode'), may hold values from -6 to 6
- patterns: float32 [16, 256, 256], P(('ty', 'tx')), may hold values from 0.2 to 3
- offsets: int32 [16, 2], P(('ty', 'tx')), may hold values from 0 to 128
- phase: float32 [256, 256], replicated, may hold values from -3.140625 to 3.140625
- past_steps: bfloat16 [5, 2, 2, 1024, 1024], P(None, None, None, 'ty', 'tx'), may hold values from -4 to 4
- past_changes: bfloat16 [5, 2, 2, 1024, 1024], P(None, None, None, 'ty', 'tx'), may hold values from -16 to 16, as said below
Outputs:
- new_object: float32 [2, 2, 1024, 1024], P(None, None, 'ty', 'tx')
- gradient: float32 [2, 2, 1024, 1024], P(None, None, 'ty', 'tx')
Inputs may be any that keep to these rules, and one draw needn't show every extreme that they name: Every entry of past_changes has the sign of the same entry of past_steps.
All inputs are finite; a program needn't handle non-finite values.
Results may differ from a plain program's by a relative error of at most 0.02.
Values sent between devices are 32-bit elements; how exact they have to be, the bound alone decides.
A program may use at most 64 MiB of HBM per device.

v0:
```python
import math

import jax
import jax.numpy as jnp
from jax import lax
from jax.sharding import PartitionSpec as P

MODES = 4
HALO = 64


REG_WEIGHT = 1.0


def extended_2(value, sides, width):
    for axis, dim in sides:
        size, length = (lax.axis_size(axis), value.shape[dim])
        up = [(i, (i + 1) % size) for i in range(size)]
        down = [(j, i) for i, j in up]
        last = lax.slice_in_dim(value, length - width, length, axis=dim)
        first = lax.slice_in_dim(value, 0, width, axis=dim)
        before = lax.ppermute(last, axis, up)
        after = lax.ppermute(first, axis, down)
        value = jnp.concatenate([before, value, after], axis=dim)
    return value


def dft_tables(length):
    indices = jnp.arange(length, dtype=jnp.int32)
    products = indices[:, None] * indices[None, :] % length
    angles = products.astype(jnp.float32) * (2.0 * math.pi / length)
    cosine_table = jnp.cos(angles) / math.sqrt(length)
    sine_table = jnp.sin(angles) / math.sqrt(length)
    forward_right = jnp.concatenate(
        [
            jnp.concatenate([cosine_table, -sine_table], 1),
            jnp.concatenate([sine_table, cosine_table], 1),
        ],
        0,
    )
    inverse_right = jnp.concatenate(
        [
            jnp.concatenate([cosine_table, sine_table], 1),
            jnp.concatenate([-sine_table, cosine_table], 1),
        ],
        0,
    )
    left_table = jnp.concatenate([cosine_table, sine_table], 0)
    return (
        forward_right.astype(jnp.bfloat16),
        inverse_right.astype(jnp.bfloat16),
        left_table.astype(jnp.bfloat16),
    )


def transform(wavefield, tables, inverse):
    right_table = tables[1] if inverse else tables[0]
    sign_value = -1.0 if inverse else 1.0
    lead_shape = wavefield.shape[:-2]
    length = wavefield.shape[-2]
    flat_wave = wavefield.reshape(-1, 2 * length).astype(jnp.bfloat16)
    first_pass = jnp.dot(flat_wave, right_table, preferred_element_type=jnp.float32)
    first_pass = first_pass.reshape(-1, length, 2 * length).astype(jnp.bfloat16)
    second_pass = jnp.einsum(
        "jk,bkl->bjl", tables[2], first_pass, preferred_element_type=jnp.float32
    )
    upper = second_pass[:, :length]
    lower = second_pass[:, length:]
    real_part = upper[:, :, :length] + sign_value * lower[:, :, length:]
    imag_part = upper[:, :, length:] - sign_value * lower[:, :, :length]
    return jnp.concatenate([real_part, imag_part], -1).reshape(lead_shape + (length, 2 * length))


def complex_product(first, second, conjugate_first):
    length = first.shape[-1] // 2
    first_real = first[..., :length]
    first_imag = first[..., length:]
    if conjugate_first:
        first_imag = -first_imag
    second_real = second[..., :length]
    second_imag = second[..., length:]
    return jnp.concatenate(
        [
            first_real * second_real - first_imag * second_imag,
            first_real * second_imag + first_imag * second_real,
        ],
        -1,
    )


def propagate(wavefield, kernel, tables, adjoint):
    spectrum = transform(wavefield, tables, False)
    spectrum = complex_product(kernel, spectrum, adjoint)
    return transform(spectrum, tables, True)


def forward_waves(windows, probe, kernel, tables):
    slice_count = windows.shape[1]
    wavefield = probe[None]
    entering = []
    for slice_index in range(slice_count):
        entering.append(wavefield)
        wavefield = complex_product(windows[:, slice_index][:, None], wavefield, False)
        if slice_index + 1 < slice_count:
            wavefield = propagate(wavefield, kernel, tables, False)
    return (transform(wavefield, tables, False), entering)


def window_gradients(far_field, entering, windows, residual, kernel, tables):
    slice_count = windows.shape[1]
    doubled = jnp.concatenate([residual, residual], -1)[:, None]
    adjoint_wave = transform(2.0 / MODES * doubled * far_field, tables, True)
    pieces = []
    for slice_index in reversed(range(slice_count)):
        pieces.append(jnp.sum(complex_product(entering[slice_index], adjoint_wave, True), axis=1))
        if slice_index > 0:
            adjoint_wave = complex_product(windows[:, slice_index][:, None], adjoint_wave, True)
            adjoint_wave = propagate(adjoint_wave, kernel, tables, True)
    return jnp.stack(pieces[::-1], 1)


def inner_product(first, second):
    return jnp.sum(first.astype(jnp.float32) * second.astype(jnp.float32))


def global_sums(values):
    return lax.psum(values, ("ty", "tx", "mode"))


def direction_search(gradient, past_steps, past_changes, portion):
    memory = past_steps.shape[0]
    step_parts = portion(past_steps)
    change_parts = portion(past_changes)
    search = gradient
    alphas = [None] * memory
    curvatures = None
    scaling = None
    for history_index in reversed(range(memory)):
        local_terms = [inner_product(step_parts[history_index], portion(search))]
        if history_index == memory - 1:
            local_terms = local_terms + [
                inner_product(step_parts[other_index], change_parts[other_index])
                for other_index in range(memory)
            ]
            local_terms = local_terms + [
                inner_product(change_parts[history_index], change_parts[history_index])
            ]
        totals = global_sums(jnp.stack(local_terms))
        if history_index == memory - 1:
            curvatures = totals[1 : memory + 1]
            scaling = totals[memory] / totals[memory + 1]
        alphas[history_index] = totals[0] / curvatures[history_index]
        search = search - alphas[history_index] * past_changes[history_index].astype(jnp.float32)
    search = scaling * search
    for history_index in range(memory):
        totals = global_sums(
            jnp.stack([inner_product(change_parts[history_index], portion(search))])
        )
        beta_value = totals[0] / curvatures[history_index]
        search = search + (alphas[history_index] - beta_value) * past_steps[history_index].astype(
            jnp.float32
        )
    return search


def per_device(object_field, probe, patterns, offsets, phase, past_steps, past_changes):
    slice_count = object_field.shape[0]
    tile_edge = object_field.shape[2]
    probe_edge = probe.shape[1]
    mode_index = lax.axis_index("mode")
    mode_count = lax.axis_size("mode")
    tables = dft_tables(probe_edge)
    kernel = jnp.concatenate([jnp.cos(phase), jnp.sin(phase)], -1)
    extended = extended_2(object_field, (("ty", 2), ("tx", 3)), HALO)
    pattern_index = 0
    starts = (0, 0, offsets[pattern_index, 0], offsets[pattern_index, 1])
    window = lax.dynamic_slice(extended, starts, (slice_count, 2, probe_edge, probe_edge))
    window_list = [jnp.concatenate([window[:, 0], window[:, 1]], -1)]
    windows = jnp.stack(window_list, 0)
    far_field, entering = forward_waves(windows, probe, kernel, tables)
    partial_intensity = jnp.sum(
        far_field[..., :probe_edge] ** 2 + far_field[..., probe_edge:] ** 2, axis=1
    )
    intensity = lax.psum(partial_intensity, "mode") / MODES
    residual = intensity - patterns
    pieces = window_gradients(far_field, entering, windows, residual, kernel, tables)
    extended_edge = tile_edge + 2 * HALO
    collected = jnp.zeros((slice_count, 2, extended_edge, extended_edge), jnp.float32)
    pattern_index = 0
    piece_now = pieces[pattern_index]
    unpacked = jnp.stack([piece_now[..., :probe_edge], piece_now[..., probe_edge:]], 1)
    starts = (0, 0, offsets[pattern_index, 0], offsets[pattern_index, 1])
    collected = lax.dynamic_update_slice(collected, unpacked, starts)
    returned = extended_2(collected, (("ty", 2), ("tx", 3)), HALO)
    columns = returned[..., 2 * HALO : 2 * HALO + tile_edge]
    columns = columns.at[..., :HALO].add(returned[..., :HALO])
    columns = columns.at[..., tile_edge - HALO :].add(returned[..., extended_edge + HALO :])
    tile_gradient = columns[:, :, 2 * HALO : 2 * HALO + tile_edge, :]
    tile_gradient = tile_gradient.at[:, :, :HALO].add(columns[:, :, :HALO])
    tile_gradient = tile_gradient.at[:, :, tile_edge - HALO :].add(
        columns[:, :, extended_edge + HALO :]
    )
    share_rows = tile_edge // mode_count

    def own_rows(array):
        return lax.dynamic_slice_in_dim(array, mode_index * share_rows, share_rows, array.ndim - 2)

    gradient = lax.psum(tile_gradient, "mode") + REG_WEIGHT * object_field
    search = direction_search(gradient, past_steps, past_changes, own_rows)
    return (object_field - search, gradient)


def solution(mesh):
    placed = (
        P(None, None, "ty", "tx"),
        P("mode", None, None),
        P(("ty", "tx"), None, None),
        P(("ty", "tx"), None),
        P(),
        P(None, None, None, "ty", "tx"),
        P(None, None, None, "ty", "tx"),
    )
    return jax.shard_map(
        per_device,
        mesh=mesh,
        in_specs=placed,
        out_specs=(P(None, None, "ty", "tx"), P(None, None, "ty", "tx")),
        check_vma=False,
    )
```

profile of v0, /device:TPU:0, one launch (start us, length us, event | category | flops | bytes accessed | tf_op | source)
XLA Modules:
  0.0 706.0 jit_solution(17379653557706497059)
XLA Ops:
  9.5 2.0 collective-permute-start.1
  14.6 6.6 collective-permute-done
  21.2 2.5 collective-permute-done.1
  26.5 2.2 collective-permute-start.3
  28.8 1.9 fusion.96
  35.5 3.4 collective-permute-done.2
  39.0 7.8 %collective-permute-done.3 = f32[2,2,384,64]{2,3,1,0:T(8,128)} collective-permute-done((f32[2,2,384,64]{2,3,1,0:T(8,128)}, f32[2,2,384,64]{2,3,1,0:T(8,128)}, u32[]{:S(2)}, u32[]{:S(2)}) %collective-permute-start.3) | collective-permute-done | bytes 393248 | tf_op jit(solution)/shard_map/ppermute | solution.py:23
  49.5 3.3 convolution_bitcast_fusion.5
  55.4 2.2 convolution_bitcast_fusion.2
  57.6 2.5 fusion.34
  63.3 3.3 convolution_bitcast_fusion.4
  70.2 1.8 copy.62
  71.9 1.8 copy.68
  73.7 1.8 copy.66
  75.5 17.9 %all-reduce.3.cloned.1.call-done = f32[1,256,256]{1,2,0:T(8,128)} async-done(((f32[1,256,256]{1,2,0:T(8,128)}), f32[1,256,256]{1,2,0:T(8,128)}) %all-reduce.3.cloned.1.call-update) | async-done | bytes 262160 | tf_op jit(solution)/shard_map/psum | solution.py:184
  95.3 3.6 convolution_bitcast_fusion.1
  101.9 3.4 convolution_bitcast_fusion.3
  108.0 2.2 convolution_bitcast_fusion
  114.1 13.8 %dynamic_update_slice.3 = f32[2,2,384,384]{3,2,1,0:T(8,128)S(1)} dynamic-update-slice(f32[2,2,384,384]{3,2,1,0:T(8,128)S(1)} %broadcast_in_dim.4, f32[2,2,256,256]{3,2,1,0:T(8,128)S(1)} %copy.74, s32[]{:T(128)} %constant.132.clone.1, s32[]{:T(128)} %constant.132.clone.1, s32[]{:T(128)S(6)} %select_n.48, s32[]{:T(128)S(6)} %select_n.49) | dynamic-update-slice | bytes 2097156 | tf_op jit(solution)/shard_map/dynamic_update_slice | solution.py:193
  129.9 6.1 collective-permute-done.4
  136.1 2.7 collective-permute-done.5
  138.7 1.9 pad_maximum_fusion
  142.3 2.4 copy.75
  144.6 3.5 collective-permute-start.6
  148.2 2.3 copy.77
  151.1 2.0 slice.597
  153.1 8.8 %collective-permute-done.6 = f32[2,2,512,64]{2,3,1,0:T(8,128)} collective-permute-done((f32[2,2,512,64]{2,3,1,0:T(8,128)}, f32[2,2,512,64]{2,3,1,0:T(8,128)}, u32[]{:S(2)}, u32[]{:S(2)}) %collective-permute-start.6) | collective-permute-done | bytes 524320 | tf_op jit(solution)/shard_map/ppermute | solution.py:22
  161.9 2.4 copy.76
  164.2 2.5 slice_add_fusion.1
  166.8 6.1 scatter-add.14
  173.1 2.5 copy.78
  175.6 1.9 slice_add_fusion
  177.4 5.8 scatter-add.15
  186.8 49.0 %all-reduce.5.cloned.1.call-done = f32[2,2,256,256]{3,2,1,0:T(8,128)} async-done(((f32[2,2,256,256]{3,2,1,0:T(8,128)}), f32[2,2,256,256]{3,2,1,0:T(8,128)}) %all-reduce.5.cloned.1.call-update) | async-done | bytes 1048592 | tf_op jit(solution)/shard_map/psum | solution.py:208
  238.4 2.4 fusion.24
  240.8 4.5 stack.86
  245.3 39.3 %psum.86 = f32[7]{0:T(128)S(1)} all-reduce(f32[7]{0:T(128)S(1)} %stack.86), channel_id=1, replica_groups=mesh['ty'=4,'tx'=4,'mode'=2] {'ty','tx','mode'}, use_global_device_ids=true, to_apply=%region_12.13 | all-reduce | flops 7 | bytes 56 | tf_op jit(solution)/shard_map/psum | solution.py:127
  290.4 1.8 fusion.8
  292.1 41.4 %psum.87 = f32[1]{0:T(128)} all-reduce(f32[1]{0:T(128)} %bitcast.61), channel_id=1, replica_groups=mesh['ty'=4,'tx'=4,'mode'=2] {'ty','tx','mode'}, use_global_device_ids=true, to_apply=%region_14.15 | all-reduce | flops 1 | bytes 8 | tf_op jit(solution)/shard_map/psum | solution.py:127
  338.9 39.5 %psum.88 = f32[1]{0:T(128)} all-reduce(f32[1]{0:T(128)} %bitcast.65), channel_id=1, replica_groups=mesh['ty'=4,'tx'=4,'mode'=2] {'ty','tx','mode'}, use_global_device_ids=true, to_apply=%region_16.17 | all-reduce | flops 1 | bytes 8 | tf_op jit(solution)/shard_map/psum | solution.py:127
  383.9 41.5 %psum.89 = f32[1]{0:T(128)} all-reduce(f32[1]{0:T(128)} %bitcast.69), channel_id=1, replica_groups=mesh['ty'=4,'tx'=4,'mode'=2] {'ty','tx','mode'}, use_global_device_ids=true, to_apply=%region_18.19 | all-reduce | flops 1 | bytes 8 | tf_op jit(solution)/shard_map/psum | solution.py:127
  430.7 39.6 %psum.90 = f32[1]{0:T(128)} all-reduce(f32[1]{0:T(128)} %bitcast.73), channel_id=1, replica_groups=mesh['ty'=4,'tx'=4,'mode'=2] {'ty','tx','mode'}, use_global_device_ids=true, to_apply=%region_20.21 | all-reduce | flops 1 | bytes 8 | tf_op jit(solution)/shard_map/psum | solution.py:127
  474.6 41.3 %psum.91 = f32[1]{0:T(128)} all-reduce(f32[1]{0:T(128)} %bitcast.77), channel_id=1, replica_groups=mesh['ty'=4,'tx'=4,'mode'=2] {'ty','tx','mode'}, use_global_device_ids=true, to_apply=%region_22.23 | all-reduce | flops 1 | bytes 8 | tf_op jit(solution)/shard_map/psum | solution.py:127
  520.5 39.5 %psum.92 = f32[1]{0:T(128)} all-reduce(f32[1]{0:T(128)} %bitcast.81), channel_id=1, replica_groups=mesh['ty'=4,'tx'=4,'mode'=2] {'ty','tx','mode'}, use_global_device_ids=true, to_apply=%region_24.25 | all-reduce | flops 1 | bytes 8 | tf_op jit(solution)/shard_map/psum | solution.py:127
  564.5 41.3 %psum.93 = f32[1]{0:T(128)} all-reduce(f32[1]{0:T(128)} %bitcast.85), channel_id=1, replica_groups=mesh['ty'=4,'tx'=4,'mode'=2] {'ty','tx','mode'}, use_global_device_ids=true, to_apply=%region_26.27 | all-reduce | flops 1 | bytes 8 | tf_op jit(solution)/shard_map/psum | solution.py:127
  610.4 39.5 %psum.94 = f32[1]{0:T(128)} all-reduce(f32[1]{0:T(128)} %bitcast.89), channel_id=1, replica_groups=mesh['ty'=4,'tx'=4,'mode'=2] {'ty','tx','mode'}, use_global_device_ids=true, to_apply=%region_28.29 | all-reduce | flops 1 | bytes 8 | tf_op jit(solution)/shard_map/psum | solution.py:127
  653.6 41.4 %psum.95 = f32[1]{0:T(128)} all-reduce(f32[1]{0:T(128)} %bitcast.92), channel_id=1, replica_groups=mesh['ty'=4,'tx'=4,'mode'=2] {'ty','tx','mode'}, use_global_device_ids=true, to_apply=%region_30.31 | all-reduce | flops 1 | bytes 8 | tf_op jit(solution)/shard_map/psum | solution.py:127
  696.4 2.8 fusion.4
  (128 shorter events, 73.6 us)
Async XLA Ops:
  7.2 4.3 copy-start.23
  7.2 86.3 %all-reduce.3.cloned.1.call-start = ((), (), s32[]{:S(2)}) async-start(), calls=%async_computation | async-start | bytes 524288 | tf_op jit(solution)/shard_map/psum | solution.py:184
  9.0 12.2 %collective-permute-start = (f32[2,2,64,256]{2,3,1,0:T(8,128)S(1)}, f32[2,2,64,256]{2,3,1,0:T(8,128)S(1)}, u32[]{:S(2)}, u32[]{:S(2)}) collective-permute-start(f32[2,2,64,256]{2,3,1,0:T(8,128)S(1)} %get-tuple-element.102), channel_id=1, source_target_pairs={{0,8},{8,16},{16,24},{24,0},{1,9},{9,17},{17,25},{25,1},{2,10},{10... | collective-permute-start | bytes 786440 | tf_op jit(solution)/shard_map/ppermute | solution.py:22
  9.5 14.2 %collective-permute-start.1 = (f32[2,2,64,256]{2,3,1,0:T(8,128)S(1)}, f32[2,2,64,256]{2,3,1,0:T(8,128)S(1)}, u32[]{:S(2)}, u32[]{:S(2)}) collective-permute-start(f32[2,2,64,256]{2,3,1,0:T(8,128)S(1)} %get-tuple-element.103), channel_id=1, source_target_pairs={{8,0},{16,8},{24,16},{0,24},{9,1},{17,9},{25,17},{1,25},{10,2},{18... | collective-permute-start | bytes 786440 | tf_op jit(solution)/shard_map/ppermute | solution.py:23
  24.9 14.1 %collective-permute-start.2 = (f32[2,2,384,64]{2,3,1,0:T(8,128)}, f32[2,2,384,64]{2,3,1,0:T(8,128)S(1)}, u32[]{:S(2)}, u32[]{:S(2)}) collective-permute-start(f32[2,2,384,64]{2,3,1,0:T(8,128)} %get-tuple-element.80), channel_id=1, source_target_pairs={{0,2},{2,4},{4,6},{6,0},{1,3},{3,5},{5,7},{7,1},{8,10},{10,12},{12... | collective-permute-start | bytes 1179656 | tf_op jit(solution)/shard_map/ppermute | solution.py:22
  26.5 20.3 %collective-permute-start.3 = (f32[2,2,384,64]{2,3,1,0:T(8,128)}, f32[2,2,384,64]{2,3,1,0:T(8,128)}, u32[]{:S(2)}, u32[]{:S(2)}) collective-permute-start(f32[2,2,384,64]{2,3,1,0:T(8,128)} %get-tuple-element.79), channel_id=1, source_target_pairs={{2,0},{4,2},{6,4},{0,6},{3,1},{5,3},{7,5},{1,7},{10,8},{12,10},{14... | collective-permute-start | bytes 1179656 | tf_op jit(solution)/shard_map/ppermute | solution.py:23
  48.0 1.3 copy-start.13
  48.1 1.4 copy-start.18
  54.5 0.9 copy-start.19
  54.5 1.0 copy-start.21
  68.3 0.9 copy-start.15
  69.2 166.6 %all-reduce.5.cloned.1.call-start = ((), (), s32[]{:S(2)}) async-start(), calls=%async_computation.1 | async-start | bytes 2097152 | tf_op jit(solution)/shard_map/psum | solution.py:208
  98.9 1.8 copy-start.16
  105.3 1.8 copy-start.17
  107.0 0.9 copy-start.20
  107.0 1.0 copy-start.22
  112.0 1.1 copy-start.14
  127.9 8.2 %copy-start = (f32[2,2,384,384]{3,2,1,0:T(8,128)}, f32[2,2,384,384]{3,2,1,0:T(8,128)S(1)}, u32[]{:S(2)}) copy-start(f32[2,2,384,384]{3,2,1,0:T(8,128)S(1)} %dynamic_update_slice.3) | copy-start | bytes 7077892
  128.0 8.1 %collective-permute-start.4 = (f32[2,2,64,384]{3,2,1,0:T(8,128)S(1)}, f32[2,2,64,384]{3,2,1,0:T(8,128)S(1)}, u32[]{:S(2)}, u32[]{:S(2)}) collective-permute-start(f32[2,2,64,384]{3,2,1,0:T(8,128)S(1)} %get-tuple-element.61), channel_id=1, source_target_pairs={{0,8},{8,16},{16,24},{24,0},{1,9},{9,17},{17,25},{25,1},{2,10},{10... | collective-permute-start | bytes 1179656 | tf_op jit(solution)/shard_map/ppermute | solution.py:22
  129.6 9.1 %collective-permute-start.5 = (f32[2,2,64,384]{3,2,1,0:T(8,128)S(1)}, f32[2,2,64,384]{3,2,1,0:T(8,128)S(1)}, u32[]{:S(2)}, u32[]{:S(2)}) collective-permute-start(f32[2,2,64,384]{3,2,1,0:T(8,128)S(1)} %get-tuple-element.62), channel_id=1, source_target_pairs={{8,0},{16,8},{24,16},{0,24},{9,1},{17,9},{25,17},{1,25},{10,2},{18... | collective-permute-start | bytes 1179656 | tf_op jit(solution)/shard_map/ppermute | solution.py:23
  144.6 17.3 %collective-permute-start.6 = (f32[2,2,512,64]{2,3,1,0:T(8,128)}, f32[2,2,512,64]{2,3,1,0:T(8,128)}, u32[]{:S(2)}, u32[]{:S(2)}) collective-permute-start(f32[2,2,512,64]{2,3,1,0:T(8,128)} %copy.75), channel_id=1, source_target_pairs={{0,2},{2,4},{4,6},{6,0},{1,3},{3,5},{5,7},{7,1},{8,10},{10,12},{12... | collective-permute-start | bytes 1572872 | tf_op jit(solution)/shard_map/ppermute | solution.py:22
  150.5 22.6 %collective-permute-start.7 = (f32[2,2,512,64]{2,3,1,0:T(8,128)}, f32[2,2,512,64]{2,3,1,0:T(8,128)}, u32[]{:S(2)}, u32[]{:S(2)}) collective-permute-start(f32[2,2,512,64]{2,3,1,0:T(8,128)} %copy.77), channel_id=1, source_target_pairs={{2,0},{4,2},{6,4},{0,6},{3,1},{5,3},{7,5},{1,7},{10,8},{12,10},{14... | collective-permute-start | bytes 1572872 | tf_op jit(solution)/shard_map/ppermute | solution.py:23
  172.9 4.5 copy-start.1
  186.7 51.7 %copy-start.2 = (bf16[5,2,2,256,256]{4,3,2,1,0:T(8,128)(2,1)S(1)}, bf16[5,2,2,256,256]{4,3,2,1,0:T(8,128)(2,1)}, u32[]{:S(2)}) copy-start(bf16[5,2,2,256,256]{4,3,2,1,0:T(8,128)(2,1)} %param.21) | copy-start | bytes 7864324
  237.4 1.0 copy-start.3
  289.4 1.0 copy-start.11
  336.1 1.0 copy-start.9
  381.1 1.0 copy-start.10
  427.9 1.0 copy-start.8
  472.9 1.0 copy-start.7
  518.8 1.0 copy-start.4
  562.8 1.0 copy-start.5
  608.6 1.0 copy-start.6
  652.7 1.0 copy-start.12
Sparse Core Ops, SparseCore 0:
  69.3 24.0 all-reduce.2
  186.9 48.8 all-reduce.4
where the time goes:
time: 708 us; the launch traced here: 706 us
  blocking collectives  404 us (57%)
  waiting for transfers between devices  105 us (15%)
  local copies, waits for them, and re-layouts  68.2 us (10%)
  other arithmetic  65 us (9%)
  between operations  32.9 us (5%)
  matrix products  17.9 us (3%)
  starting transfers between devices  12.7 us (2%)
    psum x10, blocking collectives, global_sums(): return lax.psum(values, ('ty', 'tx', 'mode'))  404 us
    psum x1, waiting for transfers between devices, per_device(): gradient = lax.psum(tile_gradient, 'mode') + REG_WEIGHT * object_field  49 us
    ppermute x4, waiting for transfers between devices, extended_2(): before = lax.ppermute(last, axis, up)  25 us
    psum x1, waiting for transfers between devices, per_device(): intensity = lax.psum(partial_intensity, 'mode') / MODES  17.9 us
    dot_general x6, matrix products, transform(): jnp.einsum('jk,bkl->bjl', tables[2], first_pass, preferred_element_type=j...  17.9 us
    unnamed x52, local copies, waits for them, and re-layouts  14.7 us
  transfers between devices with their start and end apart: 10, of which 10 were waited for; matrix products, arithmetic and copies ran while one was open for 4% of the time, Pallas kernels for 0%

commit v1 on v0

--- a/solution.py
+++ b/solution.py
@@ -112,7 +112,8 @@
     adjoint_wave = transform(2.0 / MODES * doubled * far_field, tables, True)
     pieces = []
     for slice_index in reversed(range(slice_count)):
-        pieces.append(jnp.sum(complex_product(entering[slice_index], adjoint_wave, True), axis=1))
+        piece = jnp.sum(complex_product(entering[slice_index], adjoint_wave, True), axis=1)
+        pieces.append(axis_sum(piece, "mode"))
         if slice_index > 0:
             adjoint_wave = complex_product(windows[:, slice_index][:, None], adjoint_wave, True)
             adjoint_wave = propagate(adjoint_wave, kernel, tables, True)
@@ -123,43 +124,78 @@
     return jnp.sum(first.astype(jnp.float32) * second.astype(jnp.float32))
 
 
+def axis_sum(value, axis):
+    size = lax.axis_size(axis)
+    if size & (size - 1):
+        return lax.psum(value, axis)
+    step = 1
+    while step < size:
+        pairs = [(i, i ^ step) for i in range(size)]
+        value = value + lax.ppermute(value, axis, pairs)
+        step *= 2
+    return value
+
+
 def global_sums(values):
-    return lax.psum(values, ("ty", "tx", "mode"))
+    for axis in ("mode", "ty", "tx"):
+        values = axis_sum(values, axis)
+    return values
+
+
+def folded(value, axis, dim, width):
+    size, length = (lax.axis_size(axis), value.shape[dim])
+    up = [(i, (i + 1) % size) for i in range(size)]
+    down = [(j, i) for i, j in up]
+    first = lax.slice_in_dim(value, 0, width, axis=dim)
+    last = lax.slice_in_dim(value, length - width, length, axis=dim)
+    from_before = lax.ppermute(last, axis, up)
+    from_after = lax.ppermute(first, axis, down)
+    inner = lax.slice_in_dim(value, width, length - width, axis=dim)
+    edge = inner.shape[dim]
+    head = lax.slice_in_dim(inner, 0, width, axis=dim) + from_before
+    middle = lax.slice_in_dim(inner, width, edge - width, axis=dim)
+    tail = lax.slice_in_dim(inner, edge - width, edge, axis=dim) + from_after
+    return jnp.concatenate([head, middle, tail], axis=dim)
 
 
 def direction_search(gradient, past_steps, past_changes, portion):
     memory = past_steps.shape[0]
-    step_parts = portion(past_steps)
-    change_parts = portion(past_changes)
+    steps = portion(past_steps).astype(jnp.float32)
+    changes = portion(past_changes).astype(jnp.float32)
+    part = portion(gradient)
+    cells = (1, 2, 3, 4)
+    terms = []
+    for index in range(memory):
+        terms.append(jnp.sum(steps[index][None] * changes, axis=cells))
+    for index in range(memory):
+        terms.append(jnp.sum(changes[index][None] * changes, axis=cells))
+    terms.append(jnp.sum(steps * part[None], axis=cells))
+    terms.append(jnp.sum(changes * part[None], axis=cells))
+    totals = global_sums(jnp.stack(terms))
+    cross, square = (totals[:memory], totals[memory : 2 * memory])
+    with_steps, with_changes = (totals[2 * memory], totals[2 * memory + 1])
+    alphas = [None] * memory
+    for i in reversed(range(memory)):
+        value = with_steps[i]
+        for j in reversed(range(i + 1, memory)):
+            value = value - alphas[j] * cross[i, j]
+        alphas[i] = value / cross[i, i]
+    scaling = cross[memory - 1, memory - 1] / square[memory - 1, memory - 1]
+    gammas = []
+    for i in range(memory):
+        value = with_changes[i]
+        for j in reversed(range(memory)):
+            value = value - alphas[j] * square[j, i]
+        value = scaling * value
+        for j in range(i):
+            value = value + gammas[j] * cross[j, i]
+        gammas.append(alphas[i] - value / cross[i, i])
     search = gradient
-    alphas = [None] * memory
-    curvatures = None
-    scaling = None
-    for history_index in reversed(range(memory)):
-        local_terms = [inner_product(step_parts[history_index], portion(search))]
-        if history_index == memory - 1:
-            local_terms = local_terms + [
-                inner_product(step_parts[other_index], change_parts[other_index])
-                for other_index in range(memory)
-            ]
-            local_terms = local_terms + [
-                inner_product(change_parts[history_index], change_parts[history_index])
-            ]
-        totals = global_sums(jnp.stack(local_terms))
-        if history_index == memory - 1:
-            curvatures = totals[1 : memory + 1]
-            scaling = totals[memory] / totals[memory + 1]
-        alphas[history_index] = totals[0] / curvatures[history_index]
-        search = search - alphas[history_index] * past_changes[history_index].astype(jnp.float32)
+    for i in reversed(range(memory)):
+        search = search - alphas[i] * past_changes[i].astype(jnp.float32)
     search = scaling * search
-    for history_index in range(memory):
-        totals = global_sums(
-            jnp.stack([inner_product(change_parts[history_index], portion(search))])
-        )
-        beta_value = totals[0] / curvatures[history_index]
-        search = search + (alphas[history_index] - beta_value) * past_steps[history_index].astype(
-            jnp.float32
-        )
+    for i in range(memory):
+        search = search + gammas[i] * past_steps[i].astype(jnp.float32)
     return search
 
 
@@ -181,7 +217,7 @@
     partial_intensity = jnp.sum(
         far_field[..., :probe_edge] ** 2 + far_field[..., probe_edge:] ** 2, axis=1
     )
-    intensity = lax.psum(partial_intensity, "mode") / MODES
+    intensity = axis_sum(partial_intensity, "mode") / MODES
     residual = intensity - patterns
     pieces = window_gradients(far_field, entering, windows, residual, kernel, tables)
     extended_edge = tile_edge + 2 * HALO
@@ -191,21 +227,13 @@
     unpacked = jnp.stack([piece_now[..., :probe_edge], piece_now[..., probe_edge:]], 1)
     starts = (0, 0, offsets[pattern_index, 0], offsets[pattern_index, 1])
     collected = lax.dynamic_update_slice(collected, unpacked, starts)
-    returned = extended_2(collected, (("ty", 2), ("tx", 3)), HALO)
-    columns = returned[..., 2 * HALO : 2 * HALO + tile_edge]
-    columns = columns.at[..., :HALO].add(returned[..., :HALO])
-    columns = columns.at[..., tile_edge - HALO :].add(returned[..., extended_edge + HALO :])
-    tile_gradient = columns[:, :, 2 * HALO : 2 * HALO + tile_edge, :]
-    tile_gradient = tile_gradient.at[:, :, :HALO].add(columns[:, :, :HALO])
-    tile_gradient = tile_gradient.at[:, :, tile_edge - HALO :].add(
-        columns[:, :, extended_edge + HALO :]
-    )
+    tile_gradient = folded(folded(collected, "ty", 2, HALO), "tx", 3, HALO)
     share_rows = tile_edge // mode_count
 
     def own_rows(array):
         return lax.dynamic_slice_in_dim(array, mode_index * share_rows, share_rows, array.ndim - 2)
 
-    gradient = lax.psum(tile_gradient, "mode") + REG_WEIGHT * object_field
+    gradient = tile_gradient + REG_WEIGHT * object_field
     search = direction_search(gradient, past_steps, past_changes, own_rows)
     return (object_field - search, gradient)
 

time: 708 us -> 238 us (0.34)
  blocking collectives: 404 us -> 0 us
  local copies, waits for them, and re-layouts: 68.2 us -> 29.8 us
  other arithmetic: 65 us -> 38.6 us
  waiting for transfers between devices: 105 us -> 90.5 us
  between operations: 32.9 us -> 47.4 us
    psum x10 -> x0, blocking collectives: 404 us -> none  [global_sums(): return lax.psum(values, ('ty', 'tx', 'mode'))]
    ppermute x0 -> x12, waiting for transfers between devices: none -> 70.1 us  [the longest x8 29.8 us: axis_sum(): value = value + lax.ppermute(value, axis, pairs)]
    psum x2 -> x0, waiting for transfers between devices: 66.9 us -> none  [the longest x1 49 us: per_device(): gradient = lax.psum(tile_gradient, 'mode') + REG_WEIGHT * object_field]
    scatter-add x2 -> x0, local copies, waits for them, and re-layouts: 12 us -> none  [the longest x1 6.13 us: per_device(): columns = columns.at[..., :HALO].add(returned[..., :HALO])]
    reduce_sum x10 -> x1, other arithmetic: 13.4 us -> 3.64 us  [direction_search(): terms.append(jnp.sum(changes * part[None], axis=cells))]
    ppermute x4 -> x2, waiting for transfers between devices: 25 us -> 15.6 us  [extended_2(): before = lax.ppermute(last, axis, up)]
    add x7 -> x10, other arithmetic: 12 us -> 2.76 us  [the longest x2 2.14 us: folded(): head = lax.slice_in_dim(inner, 0, width, axis=dim) + from_before]
    ppermute x4 -> x2, waiting for transfers between devices: 13.1 us -> 4.75 us  [extended_2(): after = lax.ppermute(first, axis, down)]
  transfers between devices with their start and end apart: 10 -> 16, of which waited for: 10 -> 15; matrix products, arithmetic and copies ran while one was open for 4% -> 11% of each run, Pallas kernels for 0% -> 0%
where the time goes in v1:
time: 238 us; the launch traced here: 237 us
  waiting for transfers between devices  90.5 us (38%)
  between operations  47.4 us (20%)
  other arithmetic  38.6 us (16%)
  local copies, waits for them, and re-layouts  29.8 us (13%)
  matrix products  18.6 us (8%)
  starting transfers between devices  11.8 us (5%)
    ppermute x8, waiting for transfers between devices, axis_sum(): value = value + lax.ppermute(value, axis, pairs)  29.8 us
    ppermute x2, waiting for transfers between devices, folded(): from_before = lax.ppermute(last, axis, up)  23.5 us
    dot_general x6, matrix products, transform(): jnp.einsum('jk,bkl->bjl', tables[2], first_pass, preferred_element_type=j...  18.6 us
    ppermute x2, waiting for transfers between devices, folded(): from_after = lax.ppermute(first, axis, down)  16.9 us
    ppermute x2, waiting for transfers between devices, extended_2(): before = lax.ppermute(last, axis, up)  15.6 us
    dynamic_update_slice x1, local copies, waits for them, and re-layouts, per_device(): collected = lax.dynamic_update_slice(collected, unpacked, starts)  11.7 us
    add x6, other arithmetic, transform(): real_part = upper[:, :, :length] + sign_value * lower[:, :, length:]  10.2 us
    another operation x7, other arithmetic  6.56 us
  transfers between devices with their start and end apart: 16, of which 15 were waited for; matrix products, arithmetic and copies ran while one was open for 11% of the time, Pallas kernels for 0%

profile of v1, /device:TPU:0, one launch (start us, length us, event | category | flops | bytes accessed | tf_op | source)
XLA Modules:
  0.0 236.7 jit_solution(1716671380351895030)
XLA Ops:
  0.6 1.6 copy.23
  2.9 2.0 collective-permute-start.1
  8.2 6.5 %collective-permute-done = f32[2,2,64,256]{2,3,1,0:T(8,128)S(1)} collective-permute-done((f32[2,2,64,256]{2,3,1,0:T(8,128)S(1)}, f32[2,2,64,256]{2,3,1,0:T(8,128)S(1)}, u32[]{:S(2)}, u32[]{:S(2)}) %collective-permute-start) | collective-permute-done | bytes 262176 | tf_op jit(solution)/shard_map/ppermute | solution.py:22
  14.7 2.5 %collective-permute-done.1 = f32[2,2,64,256]{2,3,1,0:T(8,128)S(1)} collective-permute-done((f32[2,2,64,256]{2,3,1,0:T(8,128)S(1)}, f32[2,2,64,256]{2,3,1,0:T(8,128)S(1)}, u32[]{:S(2)}, u32[]{:S(2)}) %collective-permute-start.1) | collective-permute-done | bytes 262176 | tf_op jit(solution)/shard_map/ppermute | solution.py:23
  17.2 1.2 pad_maximum_fusion.7
  18.4 3.6 %collective-permute-start.3 = (f32[2,2,384,64]{2,3,1,0:T(8,128)}, f32[2,2,384,64]{2,3,1,0:T(8,128)}, u32[]{:S(2)}, u32[]{:S(2)}) collective-permute-start(f32[2,2,384,64]{2,3,1,0:T(8,128)} %get-tuple-element.42), channel_id=1, source_target_pairs={{2,0},{4,2},{6,4},{0,6},{3,1},{5,3},{7,5},{1,7},{10,8},{12,10},{14... | collective-permute-start | bytes 1179656 | tf_op jit(solution)/shard_map/ppermute | solution.py:23
  23.9 1.6 copy.21
  27.8 1.8 negate_convert_fusion
  29.6 2.3 collective-permute-done.3
  31.8 9.1 %collective-permute-done.2 = f32[2,2,384,64]{2,3,1,0:T(8,128)} collective-permute-done((f32[2,2,384,64]{2,3,1,0:T(8,128)}, f32[2,2,384,64]{2,3,1,0:T(8,128)}, u32[]{:S(2)}, u32[]{:S(2)}) %collective-permute-start.2) | collective-permute-done | bytes 393248 | tf_op jit(solution)/shard_map/ppermute | solution.py:22
  41.0 2.3 fusion.12
  44.4 2.1 convolution_bitcast_fusion.5
  46.5 1.7 slice_add_fusion.4
  49.2 3.2 %convolution_bitcast_fusion.4 = f32[2,512,512]{1,2,0:T(8,128)} fusion(bf16[1,2,256,256]{2,3,1,0:T(8,128)(2,1)} %get-tuple-element.53, bf16[1,2,256,256]{2,3,1,0:T(8,128)(2,1)S(1)} %get-tuple-element.52, bf16[256,256]{1,0:T(8,128)(2,1)} %get-tuple-element.124, bf16[256,256]{1,0:T(8,128)(2,1)} %get-tuple-element.123, bf16[256,256]{1,0:T(8,128)(2,1)S(1)} %fusion.59), kind=kOutput, calls=%fused_computation.32 | convolution fusion | flops 540803072 | bytes 3014656 | tf_op jit(solution)/shard_map/jk,bkl->bjl/dot_general | solution.py:64
  52.4 1.7 fusion.29
  55.0 3.2 %convolution_bitcast_fusion.3 = f32[2,512,512]{1,2,0:T(8,128)} fusion(bf16[1,2,256,256]{2,3,1,0:T(8,128)(2,1)} %get-tuple-element.51, bf16[1,2,256,256]{2,3,1,0:T(8,128)(2,1)S(1)} %get-tuple-element.50, bf16[256,256]{1,0:T(8,128)(2,1)} %get-tuple-element.124, bf16[256,256]{1,0:T(8,128)(2,1)S(1)} %fusion.59, bf16[256,256]{1,0:T(8,128)(2,1)} %get-tuple-element.123), kind=kOutput, calls=%fused_computation.31 | convolution fusion | flops 540803072 | bytes 3014656 | tf_op jit(solution)/shard_map/jk,bkl->bjl/dot_general | solution.py:64
  58.2 1.7 slice_add_fusion.3
  60.8 1.5 collective-permute-start.4
  63.1 1.8 copy.28
  64.8 1.8 copy.29
  66.6 2.7 %collective-permute-done.4 = f32[1,256,256]{1,2,0:T(8,128)} collective-permute-done((f32[1,256,256]{1,2,0:T(8,128)}, f32[1,256,256]{1,2,0:T(8,128)}, u32[]{:S(2)}, u32[]{:S(2)}) %collective-permute-start.4) | collective-permute-done | bytes 262176 | tf_op jit(solution)/shard_map/ppermute | solution.py:134
  69.3 1.2 multiply_subtract_fusion.2
  71.3 3.4 %convolution_bitcast_fusion.2 = f32[2,512,512]{1,2,0:T(8,128)} fusion(f32[2,256,256]{1,2,0:T(8,128)} %copy-done.6, f32[2,256,256]{1,2,0:T(8,128)S(1)} %get-tuple-element.36, f32[256,512]{0,1:T(8,128)} %fusion.42, bf16[256,256]{1,0:T(8,128)(2,1)} %get-tuple-element.124, bf16[256,256]{1,0:T(8,128)(2,1)} %get-tuple-element.123, bf16[256,256]{1,0:T(8,128)(2,1)S(1)} %fusion.59), kind=kOutput, calls=%fused_computation.30 | convolution fusion | flops 540540928 | bytes 4063232 | tf_op jit(solution)/shard_map/jk,bkl->bjl/dot_general | solution.py:64
  74.7 1.7 fusion.25
  76.6 1.1 subtract_convert_fusion.1
  77.7 1.6 collective-permute-start.6
  79.3 3.3 %convolution_bitcast_fusion.1 = f32[2,512,512]{1,2,0:T(8,128)} fusion(bf16[1,2,256,256]{2,3,1,0:T(8,128)(2,1)} %get-tuple-element.49, bf16[1,2,256,256]{2,3,1,0:T(8,128)(2,1)} %get-tuple-element.48, bf16[256,256]{1,0:T(8,128)(2,1)} %get-tuple-element.124, bf16[256,256]{1,0:T(8,128)(2,1)S(1)} %fusion.59, bf16[256,256]{1,0:T(8,128)(2,1)} %get-tuple-element.123), kind=kOutput, calls=%fused_computation.29 | convolution fusion | flops 540803072 | bytes 3014656 | tf_op jit(solution)/shard_map/jk,bkl->bjl/dot_general | solution.py:64
  82.5 1.7 slice_add_fusion.2
  85.3 3.3 %convolution_bitcast_fusion = f32[2,512,512]{1,2,0:T(8,128)} fusion(bf16[1,2,256,256]{2,3,1,0:T(8,128)(2,1)} %get-tuple-element.47, bf16[1,2,256,256]{2,3,1,0:T(8,128)(2,1)} %get-tuple-element.46, bf16[256,256]{1,0:T(8,128)(2,1)} %get-tuple-element.124, bf16[256,256]{1,0:T(8,128)(2,1)} %get-tuple-element.123, bf16[256,256]{1,0:T(8,128)(2,1)S(1)} %fusion.59), kind=kOutput, calls=%fused_computation.28 | convolution fusion | flops 540803072 | bytes 3014656 | tf_op jit(solution)/shard_map/jk,bkl->bjl/dot_general | solution.py:64
  88.6 1.7 fusion.23
  91.2 12.1 %collective-permute-done.5 = f32[1,256,512]{1,2,0:T(8,128)S(1)} collective-permute-done((f32[1,256,512]{1,2,0:T(8,128)S(1)}, f32[1,256,512]{1,2,0:T(8,128)S(1)}, u32[]{:S(2)}, u32[]{:S(2)}) %collective-permute-start.5) | collective-permute-done | bytes 524320 | tf_op jit(solution)/shard_map/ppermute | solution.py:134
  103.6 1.3 copy.30
  104.9 1.6 broadcast_in_dim.4
  106.5 11.7 %dynamic_update_slice.3 = f32[2,2,384,384]{3,2,1,0:T(8,128)} dynamic-update-slice(f32[2,2,384,384]{3,2,1,0:T(8,128)} %broadcast_in_dim.4, f32[2,2,256,256]{3,2,1,0:T(8,128)} %copy.30, s32[]{:T(128)} %constant.12.clone.1, s32[]{:T(128)} %constant.12.clone.1, s32[]{:T(128)S(6)} %select_n.39, s32[]{:T(128)S(6)} %select_n.40) | dynamic-update-slice | bytes 2097156 | tf_op jit(solution)/shard_map/dynamic_update_slice | solution.py:229
  118.2 1.0 slice.729
  119.3 7.2 %collective-permute-done.7 = f32[2,2,64,384]{3,2,1,0:T(8,128)S(1)} collective-permute-done((f32[2,2,64,384]{3,2,1,0:T(8,128)S(1)}, f32[2,2,64,384]{3,2,1,0:T(8,128)S(1)}, u32[]{:S(2)}, u32[]{:S(2)}) %collective-permute-start.7) | collective-permute-done | bytes 393248 | tf_op jit(solution)/shard_map/ppermute | solution.py:151
  126.5 1.9 slice_add_fusion.6
  128.4 2.1 dynamic-slice_convert_fusion
  130.6 3.4 %collective-permute-done.8 = f32[2,2,64,384]{3,2,1,0:T(8,128)S(1)} collective-permute-done((f32[2,2,64,384]{3,2,1,0:T(8,128)}, f32[2,2,64,384]{3,2,1,0:T(8,128)S(1)}, u32[]{:S(2)}, u32[]{:S(2)}) %collective-permute-start.8) | collective-permute-done | bytes 393248 | tf_op jit(solution)/shard_map/ppermute | solution.py:152
  134.8 16.3 %collective-permute-done.9 = f32[2,2,256,64]{3,2,1,0:T(8,128)S(1)} collective-permute-done((f32[2,2,256,64]{3,2,1,0:T(8,128)S(1)}, f32[2,2,256,64]{3,2,1,0:T(8,128)S(1)}, u32[]{:S(2)}, u32[]{:S(2)}) %collective-permute-start.9) | collective-permute-done | bytes 262176 | tf_op jit(solution)/shard_map/ppermute | solution.py:151
  151.7 13.5 %collective-permute-done.10 = f32[2,2,256,64]{3,2,1,0:T(8,128)S(1)} collective-permute-done((f32[2,2,256,64]{3,2,1,0:T(8,128)S(1)}, f32[2,2,256,64]{3,2,1,0:T(8,128)S(1)}, u32[]{:S(2)}, u32[]{:S(2)}) %collective-permute-start.10) | collective-permute-done | bytes 262176 | tf_op jit(solution)/shard_map/ppermute | solution.py:152
  167.4 3.6 %fusion.10 = (f32[5]{0:T(128)S(1)}, f32[5]{0:T(128)S(1)}, f32[5]{0:T(128)S(1)}, f32[5]{0:T(128)S(1)}, f32[5]{0:T(128)S(1)}, /*index=5*/f32[5]{0:T(128)S(1)}, f32...) fusion(f32[2,2,128,256]{3,2,1,0:T(8,128)S(1)} %constant_dynamic-slice_fus, ...), kind=kLoop, calls=%fused_computation.21 | loop fusion | flops 17039300 | bytes 8388852 | tf_op jit(solution)/shard_map/reduce_sum | solution.py:173
  171.7 3.1 %collective-permute-done.11 = f32[12,5]{1,0:T(8,128)S(1)} collective-permute-done((f32[12,5]{1,0:T(8,128)S(1)}, f32[12,5]{1,0:T(8,128)S(1)}, u32[]{:S(2)}, u32[]{:S(2)}) %collective-permute-start.11) | collective-permute-done | bytes 272 | tf_op jit(solution)/shard_map/ppermute | solution.py:134
  174.8 1.2 collective-permute-done.12
  176.5 3.1 %collective-permute-done.13 = f32[12,5]{1,0:T(8,128)S(1)} collective-permute-done((f32[12,5]{1,0:T(8,128)S(1)}, f32[12,5]{1,0:T(8,128)S(1)}, u32[]{:S(2)}, u32[]{:S(2)}) %collective-permute-start.13) | collective-permute-done | bytes 272 | tf_op jit(solution)/shard_map/ppermute | solution.py:134
  179.6 3.6 %collective-permute-done.14 = f32[12,5]{1,0:T(8,128)S(1)} collective-permute-done((f32[12,5]{1,0:T(8,128)S(1)}, f32[12,5]{1,0:T(8,128)S(1)}, u32[]{:S(2)}, u32[]{:S(2)}) %collective-permute-start.14) | collective-permute-done | bytes 272 | tf_op jit(solution)/shard_map/ppermute | solution.py:134
  183.9 3.9 %collective-permute-done.15 = f32[12,5]{1,0:T(8,128)S(1)} collective-permute-done((f32[12,5]{1,0:T(8,128)S(1)}, f32[12,5]{1,0:T(8,128)S(1)}, u32[]{:S(2)}, u32[]{:S(2)}) %collective-permute-start.15) | collective-permute-done | bytes 272 | tf_op jit(solution)/shard_map/ppermute | solution.py:134
  232.3 4.4 %fusion.15 = f32[2,2,256,256]{3,2,1,0:T(8,128)} fusion(f32[2,2,256,256]{3,2,1,0:T(8,128)} %param.7, f32[2,2,256,256]{3,2,1,0:T(8,128)} %copy-done.4, bf16[5,2,2,256,256]{4,3,2,1,0:T(8,128)(2,1)S(1)} %copy-done, f32[]{:T(128)S(6)} %sub.238, f32[]{:T(128)S(6)} %sub.232, f32[]{:T(128)S(6)} %sub.226, f32[]{:T(128)S(6)} %sub.220, f32[]{:T(128)S(6)} %sub.214, ...), kind=kLoop, calls=%fused_computation.59 | loop fusion | flops 8388608 | bytes 8388652 | tf_op jit(solution)/shard_map/sub | solution.py:238
  (91 shorter events, 19.6 us)
Async XLA Ops:
  0.6 4.3 %copy-start.13 = (s32[1,2]{1,0:T(1,128)S(1)}, s32[1,2]{1,0:T(1,128)}, u32[]{:S(2)}) copy-start(s32[1,2]{1,0:T(1,128)} %param.10) | copy-start | bytes 28
  2.2 19.8 %copy-start.10 = (f32[256,256]{1,0:T(8,128)S(1)}, f32[256,256]{1,0:T(8,128)}, u32[]{:S(2)}) copy-start(f32[256,256]{1,0:T(8,128)} %param.11) | copy-start | bytes 786436
  2.4 12.2 %collective-permute-start = (f32[2,2,64,256]{2,3,1,0:T(8,128)S(1)}, f32[2,2,64,256]{2,3,1,0:T(8,128)S(1)}, u32[]{:S(2)}, u32[]{:S(2)}) collective-permute-start(f32[2,2,64,256]{2,3,1,0:T(8,128)S(1)} %get-tuple-element.67), channel_id=1, source_target_pairs={{0,8},{8,16},{16,24},{24,0},{1,9},{9,17},{17,25},{25,1},{2,10},{10... | collective-permute-start | bytes 786440 | tf_op jit(solution)/shard_map/ppermute | solution.py:22
  2.9 14.2 %collective-permute-start.1 = (f32[2,2,64,256]{2,3,1,0:T(8,128)S(1)}, f32[2,2,64,256]{2,3,1,0:T(8,128)S(1)}, u32[]{:S(2)}, u32[]{:S(2)}) collective-permute-start(f32[2,2,64,256]{2,3,1,0:T(8,128)S(1)} %get-tuple-element.68), channel_id=1, source_target_pairs={{8,0},{16,8},{24,16},{0,24},{9,1},{17,9},{25,17},{1,25},{10,2},{18... | collective-permute-start | bytes 786440 | tf_op jit(solution)/shard_map/ppermute | solution.py:23
  17.2 4.8 %copy-start.5 = (f32[2,2,64,256]{2,3,1,0:T(8,128)}, f32[2,2,64,256]{2,3,1,0:T(8,128)S(1)}, u32[]{:S(2)}) copy-start(f32[2,2,64,256]{2,3,1,0:T(8,128)S(1)} %collective-permute-done.1) | copy-start | bytes 786436
  18.4 13.5 %collective-permute-start.3 = (f32[2,2,384,64]{2,3,1,0:T(8,128)}, f32[2,2,384,64]{2,3,1,0:T(8,128)}, u32[]{:S(2)}, u32[]{:S(2)}) collective-permute-start(f32[2,2,384,64]{2,3,1,0:T(8,128)} %get-tuple-element.42), channel_id=1, source_target_pairs={{2,0},{4,2},{6,4},{0,6},{3,1},{5,3},{7,5},{1,7},{10,8},{12,10},{14... | collective-permute-start | bytes 1179656 | tf_op jit(solution)/shard_map/ppermute | solution.py:23
  22.0 19.0 %collective-permute-start.2 = (f32[2,2,384,64]{2,3,1,0:T(8,128)}, f32[2,2,384,64]{2,3,1,0:T(8,128)}, u32[]{:S(2)}, u32[]{:S(2)}) collective-permute-start(f32[2,2,384,64]{2,3,1,0:T(8,128)} %get-tuple-element.43), channel_id=1, source_target_pairs={{0,2},{2,4},{4,6},{6,0},{1,3},{3,5},{5,7},{7,1},{8,10},{10,12},{12... | collective-permute-start | bytes 1179656 | tf_op jit(solution)/shard_map/ppermute | solution.py:22
  43.4 1.0 copy-start.11
  43.4 1.0 copy-start.12
  46.5 1.8 copy-start.8
  59.9 0.9 copy-start.6
  60.8 8.5 %collective-permute-start.4 = (f32[1,256,256]{1,2,0:T(8,128)}, f32[1,256,256]{1,2,0:T(8,128)}, u32[]{:S(2)}, u32[]{:S(2)}) collective-permute-start(f32[1,256,256]{1,2,0:T(8,128)} %bitcast.42), channel_id=1, source_target_pairs={{0,1},{1,0},{2,3},{3,2},{4,5},{5,4},{6,7},{7,6},{8,9},{9,8},{10,11... | collective-permute-start | bytes 786440 | tf_op jit(solution)/shard_map/ppermute | solution.py:134
  74.7 1.8 copy-start.7
  77.7 13.4 %collective-permute-start.6 = (f32[1,256,512]{1,2,0:T(8,128)S(1)}, f32[1,256,512]{1,2,0:T(8,128)S(1)}, u32[]{:S(2)}, u32[]{:S(2)}) collective-permute-start(f32[1,256,512]{1,2,0:T(8,128)S(1)} %bitcast.233), channel_id=1, source_target_pairs={{0,1},{1,0},{2,3},{3,2},{4,5},{5,4},{6,7},{7,6},{8,9},{9,8},{10,11... | collective-permute-start | bytes 1572872 | tf_op jit(solution)/shard_map/ppermute | solution.py:134
  82.5 1.8 copy-start.9
  90.5 12.7 %collective-permute-start.5 = (f32[1,256,512]{1,2,0:T(8,128)S(1)}, f32[1,256,512]{1,2,0:T(8,128)S(1)}, u32[]{:S(2)}, u32[]{:S(2)}) collective-permute-start(f32[1,256,512]{1,2,0:T(8,128)S(1)} %bitcast.234), channel_id=1, source_target_pairs={{0,1},{1,0},{2,3},{3,2},{4,5},{5,4},{6,7},{7,6},{8,9},{9,8},{10,11... | collective-permute-start | bytes 1572872 | tf_op jit(solution)/shard_map/ppermute | solution.py:134
  106.5 21.9 %copy-start = (bf16[5,2,2,256,256]{4,3,2,1,0:T(8,128)(2,1)S(1)}, bf16[5,2,2,256,256]{4,3,2,1,0:T(8,128)(2,1)}, u32[]{:S(2)}) copy-start(bf16[5,2,2,256,256]{4,3,2,1,0:T(8,128)(2,1)} %param.12) | copy-start | bytes 7864324
  119.2 7.3 %collective-permute-start.7 = (f32[2,2,64,384]{3,2,1,0:T(8,128)S(1)}, f32[2,2,64,384]{3,2,1,0:T(8,128)S(1)}, u32[]{:S(2)}, u32[]{:S(2)}) collective-permute-start(f32[2,2,64,384]{3,2,1,0:T(8,128)S(1)} %slice.729), channel_id=1, source_target_pairs={{0,8},{8,16},{16,24},{24,0},{1,9},{9,17},{17,25},{25,1},{2,10},{10... | collective-permute-start | bytes 1179656 | tf_op jit(solution)/shard_map/ppermute | solution.py:151
  128.4 5.6 %collective-permute-start.8 = (f32[2,2,64,384]{3,2,1,0:T(8,128)}, f32[2,2,64,384]{3,2,1,0:T(8,128)S(1)}, u32[]{:S(2)}, u32[]{:S(2)}) collective-permute-start(f32[2,2,64,384]{3,2,1,0:T(8,128)} %get-tuple-element.25), channel_id=1, source_target_pairs={{8,0},{16,8},{24,16},{0,24},{9,1},{17,9},{25,17},{1,25},{10,2},{18... | collective-permute-start | bytes 1179656 | tf_op jit(solution)/shard_map/ppermute | solution.py:152
  128.4 2.1 copy-start.2
  134.4 16.7 %collective-permute-start.9 = (f32[2,2,256,64]{3,2,1,0:T(8,128)S(1)}, f32[2,2,256,64]{3,2,1,0:T(8,128)S(1)}, u32[]{:S(2)}, u32[]{:S(2)}) collective-permute-start(f32[2,2,256,64]{3,2,1,0:T(8,128)S(1)} %slice.734), channel_id=1, source_target_pairs={{0,2},{2,4},{4,6},{6,0},{1,3},{3,5},{5,7},{7,1},{8,10},{10,12},{12... | collective-permute-start | bytes 786440 | tf_op jit(solution)/shard_map/ppermute | solution.py:151
  151.3 13.9 %collective-permute-start.10 = (f32[2,2,256,64]{3,2,1,0:T(8,128)S(1)}, f32[2,2,256,64]{3,2,1,0:T(8,128)S(1)}, u32[]{:S(2)}, u32[]{:S(2)}) collective-permute-start(f32[2,2,256,64]{3,2,1,0:T(8,128)S(1)} %get-tuple-element.45), channel_id=1, source_target_pairs={{2,0},{4,2},{6,4},{0,6},{3,1},{5,3},{7,5},{1,7},{10,8},{12,10},{14... | collective-permute-start | bytes 786440 | tf_op jit(solution)/shard_map/ppermute | solution.py:152
  151.6 13.7 %copy-start.3 = (f32[2,2,256,256]{3,2,1,0:T(8,128)S(1)}, f32[2,2,256,256]{3,2,1,0:T(8,128)}, u32[]{:S(2)}) copy-start(f32[2,2,256,256]{3,2,1,0:T(8,128)} %param.7) | copy-start | bytes 3145732
  165.3 2.1 copy-start.1
  165.8 1.0 copy-start.4
  171.1 3.7 %collective-permute-start.11 = (f32[12,5]{1,0:T(8,128)S(1)}, f32[12,5]{1,0:T(8,128)S(1)}, u32[]{:S(2)}, u32[]{:S(2)}) collective-permute-start(f32[12,5]{1,0:T(8,128)S(1)} %stack.79), channel_id=1, source_target_pairs={{0,1},{1,0},{2,3},{3,2},{4,5},{5,4},{6,7},{7,6},{8,9},{9,8},{10,11... | collective-permute-start | bytes 728 | tf_op jit(solution)/shard_map/ppermute | solution.py:134
  174.8 1.2 collective-permute-start.12
  176.0 3.7 %collective-permute-start.13 = (f32[12,5]{1,0:T(8,128)S(1)}, f32[12,5]{1,0:T(8,128)S(1)}, u32[]{:S(2)}, u32[]{:S(2)}) collective-permute-start(f32[12,5]{1,0:T(8,128)S(1)} %add.190), channel_id=1, source_target_pairs={{0,16},{8,24},{16,0},{24,8},{1,17},{9,25},{17,1},{25,9},{2,18},{10... | collective-permute-start | bytes 728 | tf_op jit(solution)/shard_map/ppermute | solution.py:134
  179.6 3.7 %collective-permute-start.14 = (f32[12,5]{1,0:T(8,128)S(1)}, f32[12,5]{1,0:T(8,128)S(1)}, u32[]{:S(2)}, u32[]{:S(2)}) collective-permute-start(f32[12,5]{1,0:T(8,128)S(1)} %add.191), channel_id=1, source_target_pairs={{0,2},{2,0},{4,6},{6,4},{1,3},{3,1},{5,7},{7,5},{8,10},{10,8},{12,... | collective-permute-start | bytes 728 | tf_op jit(solution)/shard_map/ppermute | solution.py:134
  183.3 4.5 %collective-permute-start.15 = (f32[12,5]{1,0:T(8,128)S(1)}, f32[12,5]{1,0:T(8,128)S(1)}, u32[]{:S(2)}, u32[]{:S(2)}) collective-permute-start(f32[12,5]{1,0:T(8,128)S(1)} %add.192), channel_id=1, source_target_pairs={{0,4},{2,6},{4,0},{6,2},{1,5},{3,7},{5,1},{7,3},{8,12},{10,14},{12... | collective-permute-start | bytes 728 | tf_op jit(solution)/shard_map/ppermute | solution.py:134
